TPU v7x, 512 devices: a whole 4x8x8 slice. The times are simulated.
512 devices in a mesh: seq: 32 (over z_lo, y, core), head: 16 (over z_hi, x).
Axes of the slice: x: 4, y: 8, z: 8 (z_hi: 4, z_lo: 2; z = z_hi * 2 + z_lo), core: 2. Of those that a mesh axis runs over, the one named last changes fastest.
Arguments:
- source_hidden: bfloat16 [8192, 2048], P('seq', 'head'), may hold values from -64 to 64
- target_hidden: bfloat16 [16384, 2048], P('seq', 'head'), may hold values from -64 to 64
- source_length: int32 [1], replicated, may hold values from 4096 to 8192
- target_length: int32 [1], replicated, may hold values from 8192 to 16384
- encoder_gain: float32 [2048], replicated, may hold values from 0.25 to 1.75
- query_weight: bfloat16 [2048, 2048], P(None, 'head'), may hold values from -1 to 1
- key_weight: bfloat16 [2048, 2048], P(None, 'head'), may hold values from -1 to 1
- value_weight: bfloat16 [2048, 2048], P(None, 'head'), may hold values from -0.5 to 0.5
- output_weight: bfloat16 [2048, 2048], P('head'), may hold values from -0.5 to 0.5
- final_gain: float32 [2048], replicated, may hold values from 0.25 to 1.75
- cross_query: bfloat16 [2048, 2048], P(None, 'head'), may hold values from -1 to 1
- cross_key: bfloat16 [2048, 2048], P(None, 'head'), may hold values from -1 to 1
- cross_value: bfloat16 [2048, 2048], P(None, 'head'), may hold values from -0.5 to 0.5
- cross_gain: float32 [2048], replicated, may hold values from 0.25 to 1.75
Outputs:
- encoder_out: bfloat16 [8192, 2048], P('seq', 'head')
- cross_context: bfloat16 [16384, 2048], P('seq', 'head')
All inputs are finite; a program needn't handle non-finite values.
Results may differ from a plain program's by a relative error of at most 0.03.
Values may be sent and summed in bfloat16 or wider, within the bound.
No kernel may reach another device: no remote copies, remote signals or barrier semaphores. Data moves between devices by JAX's collectives and lax.ppermute only.
A program may use at most 64 MiB of HBM per device.

v0:
```python
import math
import jax
import jax.numpy as jnp
from jax import lax
from jax.sharding import PartitionSpec as P

HD = 128
EPSILON = 1e-05
MASKED = -1e30


def layer_norm(hidden, scale_gain):
    floats = hidden.astype(jnp.float32)
    center = floats - jnp.mean(floats, axis=-1, keepdims=True)
    spread = jnp.mean(center * center, axis=-1, keepdims=True)
    return (center * lax.rsqrt(spread + EPSILON) * scale_gain).astype(jnp.bfloat16)


def project(normed, weight):
    return jnp.dot(normed, weight, preferred_element_type=jnp.float32).astype(jnp.bfloat16)


def make_fold(queries, key_limit):
    head_count = queries.shape[1] // HD
    row_count = queries.shape[0]
    grouped = queries.reshape(row_count, head_count, HD)

    def fold_keys(running, pieces, first_row):
        key_rows, value_rows = pieces
        key_count = key_rows.shape[0]
        block_size = math.gcd(key_count, 1024)

        def block_step(block_index, carried):
            running_max, denominator, context_sum = carried
            offset = block_index * block_size
            key_block = lax.dynamic_slice_in_dim(key_rows, offset, block_size, 0).reshape(
                block_size, head_count, HD
            )
            value_block = lax.dynamic_slice_in_dim(value_rows, offset, block_size, 0).reshape(
                block_size, head_count, HD
            )
            places = offset + lax.iota(jnp.int32, block_size)
            usable = (places < key_limit)[None, None, :]
            scores = jnp.einsum(
                "rhd,khd->hrk", grouped, key_block, preferred_element_type=jnp.float32
            ) * HD ** (-0.5)
            scores = jnp.where(usable, scores, MASKED)
            new_max = jnp.maximum(running_max, jnp.max(scores, axis=-1))
            weights = jnp.where(usable, jnp.exp(scores - new_max[:, :, None]), 0.0)
            rescale = jnp.exp(running_max - new_max)
            denominator = denominator * rescale + jnp.sum(weights, axis=-1)
            update = jnp.einsum(
                "hrk,khd->rhd",
                weights.astype(jnp.bfloat16),
                value_block,
                preferred_element_type=jnp.float32,
            )
            context_sum = context_sum * rescale.T[:, :, None] + update
            return (new_max, denominator, context_sum)

        return lax.fori_loop(0, key_count // block_size, block_step, running)

    initial = (
        jnp.full((head_count, row_count), MASKED, jnp.float32),
        jnp.zeros((head_count, row_count), jnp.float32),
        jnp.zeros((row_count, head_count, HD), jnp.float32),
    )
    return (fold_keys, initial)


def finish(running):
    running_max, denominator, context_sum = running
    row_count = context_sum.shape[0]
    return (context_sum / denominator.T[:, :, None]).reshape(row_count, -1)


def shards(
    source_hidden,
    target_hidden,
    source_length,
    target_length,
    encoder_gain,
    query_weight,
    key_weight,
    value_weight,
    output_weight,
    final_gain,
    cross_query,
    cross_key,
    cross_value,
    cross_gain,
):
    source_full, target_full = (
        lax.all_gather(source_hidden, "head", axis=1, tiled=True),
        lax.all_gather(target_hidden, "head", axis=1, tiled=True),
    )
    key_limit = source_length[0]
    source_norm = layer_norm(source_full, encoder_gain)
    queries = project(source_norm, query_weight)
    keys_local = project(source_norm, key_weight)
    values_local = project(source_norm, value_weight)
    folder, initial = make_fold(queries, key_limit)
    attended = folder(
        initial,
        (
            lax.all_gather(keys_local, "seq", axis=0, tiled=True),
            lax.all_gather(values_local, "seq", axis=0, tiled=True),
        ),
        jnp.int32(0),
    )
    encoder_context = finish(attended).astype(jnp.bfloat16)
    partial_sum = jnp.dot(encoder_context, output_weight, preferred_element_type=jnp.float32)
    share_sum = lax.psum_scatter(
        partial_sum.astype(jnp.bfloat16), "head", scatter_dimension=1, tiled=True
    ).astype(jnp.float32)
    encoder_out = (source_hidden.astype(jnp.float32) + share_sum).astype(jnp.bfloat16)
    encoder_full = lax.all_gather(encoder_out, "head", axis=1, tiled=True)
    encoder_final = layer_norm(encoder_full, final_gain)
    memory_keys = project(encoder_final, cross_key)
    memory_values = project(encoder_final, cross_value)
    target_norm = layer_norm(target_full, cross_gain)
    target_queries = project(target_norm, cross_query)
    cross_folder, cross_initial = make_fold(target_queries, key_limit)
    crossed = cross_folder(
        cross_initial,
        (
            lax.all_gather(memory_keys, "seq", axis=0, tiled=True),
            lax.all_gather(memory_values, "seq", axis=0, tiled=True),
        ),
        jnp.int32(0),
    )
    target_rows = target_hidden.shape[0]
    positions = lax.axis_index("seq") * target_rows + lax.iota(jnp.int32, target_rows)
    live_rows = (positions < target_length[0])[:, None]
    cross_context = jnp.where(live_rows, finish(crossed), 0.0).astype(jnp.bfloat16)
    return (encoder_out, cross_context)


def solution(mesh):
    in_specs = (
        P("seq", "head"),
        P("seq", "head"),
        P(),
        P(),
        P(),
        P(None, "head"),
        P(None, "head"),
        P(None, "head"),
        P("head", None),
        P(),
        P(None, "head"),
        P(None, "head"),
        P(None, "head"),
        P(),
    )
    out_specs = (P("seq", "head"), P("seq", "head"))
    return jax.shard_map(shards, mesh=mesh, in_specs=in_specs, out_specs=out_specs, check_vma=False)
```

profile of v0, /device:TPU:1, one launch (start us, length us, event | category | flops | bytes accessed | tf_op | source)
XLA Modules:
  0.0 650.4 jit_solution(5712484617599095575)
XLA Ops:
  8.0 68.6 %all-gather.8.cloned.1.call-done = bf16[256,2048]{1,0:T(8,128)(2,1)} async-done(((bf16[256,128]{1,0:T(8,128)(2,1)}), bf16[256,2048]{1,0:T(8,128)(2,1)}) %all-gather.8.cloned.1.call-update) | async-done | bytes 1048592 | tf_op jit(solution)/shard_map/all_gather | solution.py:94
  76.6 1.5 convert_reduce_fusion.2
  78.1 1.6 fusion.50
  83.0 63.3 %all-gather.10.cloned.1.call-done = bf16[8192,128]{1,0:T(8,128)(2,1)} async-done(((bf16[256,128]{1,0:T(8,128)(2,1)}), bf16[8192,128]{1,0:T(8,128)(2,1)}) %all-gather.10.cloned.1.call-update) | async-done | bytes 2097168 | tf_op jit(solution)/shard_map/all_gather | solution.py:106
  146.3 69.8 %all-gather.12.cloned.1.call-done = bf16[8192,128]{1,0:T(8,128)(2,1)} async-done(((bf16[256,128]{1,0:T(8,128)(2,1)}), bf16[8192,128]{1,0:T(8,128)(2,1)}) %all-gather.12.cloned.1.call-update) | async-done | bytes 2097168 | tf_op jit(solution)/shard_map/all_gather | solution.py:107
  216.1 29.3 %while.36 = (s32[]{:T(128)}, f32[1,256]{1,0:T(1,128)S(1)}, f32[1,256]{1,0:T(1,128)S(1)}, f32[256,1,128]{0,2,1:T(8,128)S(1)}, s32[]{:T(128)}, /*index=5*/bf16[819...) while((s32[]{:T(128)}, f32[1,256]{1,0:T(1,128)S(1)}, ...), condition=%wide.region_5.6_spmd.clone, body=%wide.region_2.5_spmd.clone.sunk | while | flops 136678656 | bytes 4018367 | solution.py:61
  247.2 89.8 %reduce-scatter.4.cloned.1.call-done = bf16[128,256]{1,0:T(8,128)(2,1)} async-done(((bf16[2048,256]{1,0:T(8,128)(2,1)}), bf16[128,256]{1,0:T(8,128)(2,1)}) %reduce-scatter.4.cloned.1.call-update) | async-done | bytes 65552
  339.3 60.9 %all-gather.14.cloned.1.call-done = bf16[256,2048]{1,0:T(8,128)(2,1)} async-done(((bf16[256,128]{1,0:T(8,128)(2,1)}), bf16[256,2048]{1,0:T(8,128)(2,1)}) %all-gather.14.cloned.1.call-update) | async-done | bytes 1048592 | tf_op jit(solution)/shard_map/all_gather | solution.py:117
  400.2 1.5 convert_reduce_fusion.1
  401.8 1.7 fusion.47
  406.7 62.5 %all-gather.18.cloned.1.call-done = bf16[512,2048]{1,0:T(8,128)(2,1)} async-done(((bf16[512,128]{1,0:T(8,128)(2,1)}), bf16[512,2048]{1,0:T(8,128)(2,1)}) %all-gather.18.cloned.1.call-update) | async-done | bytes 2097168 | tf_op jit(solution)/shard_map/all_gather | solution.py:95
  469.2 2.1 convert_reduce_fusion
  473.0 64.2 %all-gather.20.cloned.1.call-done = bf16[8192,128]{1,0:T(8,128)(2,1)} async-done(((bf16[256,128]{1,0:T(8,128)(2,1)}), bf16[8192,128]{1,0:T(8,128)(2,1)}) %all-gather.20.cloned.1.call-update) | async-done | bytes 2097168 | tf_op jit(solution)/shard_map/all_gather | solution.py:128
  537.2 70.0 %all-gather.16.cloned.1.call-done = bf16[8192,128]{1,0:T(8,128)(2,1)} async-done(((bf16[256,128]{1,0:T(8,128)(2,1)}), bf16[8192,128]{1,0:T(8,128)(2,1)}) %all-gather.16.cloned.1.call-update) | async-done | bytes 2097168 | tf_op jit(solution)/shard_map/all_gather | solution.py:127
  607.1 35.5 %while.37 = (s32[]{:T(128)}, f32[1,512]{1,0:T(1,128)S(1)}, f32[1,512]{1,0:T(1,128)S(1)}, f32[512,1,128]{0,2,1:T(8,128)S(1)}, s32[]{:T(128)}, /*index=5*/bf16[819...) while((s32[]{:T(128)}, f32[1,512]{1,0:T(1,128)S(1)}, ...), condition=%wide.region_14.15_spmd.clone, body=%wide.region_11.14_spmd.clone.sunk | while | flops 275452416 | bytes 7508159 | solution.py:61
  609.8 1.7 fusion.107
  612.2 1.4 fusion.103
  614.3 1.7 fusion.107
  618.7 1.7 fusion.107
  623.1 1.7 fusion.107
  627.6 1.7 fusion.107
  632.0 1.7 fusion.107
  636.4 1.7 fusion.107
  640.9 1.7 fusion.107
  (174 shorter events, 61.8 us)
Async XLA Ops:
  7.2 238.2 %copy-start = (bf16[128,2048]{1,0:T(8,128)(2,1)S(1)}, bf16[128,2048]{1,0:T(8,128)(2,1)}, u32[]{:S(2)}) copy-start(bf16[128,2048]{1,0:T(8,128)(2,1)} %param.26) | copy-start | bytes 1572868
  7.2 72.6 %copy-start.8 = (f32[2048]{0:T(1024)S(1)}, f32[2048]{0:T(1024)}, u32[]{:S(2)}) copy-start(f32[2048]{0:T(1024)} %param.22) | copy-start | bytes 24580
  7.2 69.4 %all-gather.8.cloned.1.call-start = ((), (), s32[]{:S(2)}) async-start(), calls=%async_computation.1 | async-start | bytes 1114112 | tf_op jit(solution)/shard_map/all_gather | solution.py:94
  7.9 72.3 %copy-start.4 = (bf16[2048,128]{1,0:T(8,128)(2,1)S(1)}, bf16[2048,128]{1,0:T(8,128)(2,1)}, u32[]{:S(2)}) copy-start(bf16[2048,128]{1,0:T(8,128)(2,1)} %param.24) | copy-start | bytes 1572868
  7.9 138.4 %all-gather.10.cloned.1.call-start = ((), (), s32[]{:S(2)}) async-start(), calls=%async_computation.2 | async-start | bytes 2162688 | tf_op jit(solution)/shard_map/all_gather | solution.py:106
  76.6 3.2 copy-start.1
  79.8 1.6 copy-start.5
  80.2 2.3 copy-start.6
  81.3 134.8 %all-gather.12.cloned.1.call-start = ((), (), s32[]{:S(2)}) async-start(), calls=%async_computation.3 | async-start | bytes 2162688 | tf_op jit(solution)/shard_map/all_gather | solution.py:107
  82.5 254.6 %reduce-scatter.4.cloned.1.call-start = ((), (), s32[]{:S(2)}) async-start(), calls=%async_computation.8 | async-start | bytes 1114112
  245.4 92.6 %copy-start.7 = (bf16[256,128]{1,0:T(8,128)(2,1)S(1)}, bf16[256,128]{1,0:T(8,128)(2,1)}, u32[]{:S(2)}) copy-start(bf16[256,128]{1,0:T(8,128)(2,1)} %param.18) | copy-start | bytes 196612
  247.2 156.3 %copy-start.9 = (bf16[2048,128]{1,0:T(8,128)(2,1)S(1)}, bf16[2048,128]{1,0:T(8,128)(2,1)}, u32[]{:S(2)}) copy-start(bf16[2048,128]{1,0:T(8,128)(2,1)} %param.30) | copy-start | bytes 1572868
  247.2 156.3 %copy-start.12 = (f32[2048]{0:T(1024)S(1)}, f32[2048]{0:T(1024)}, u32[]{:S(2)}) copy-start(f32[2048]{0:T(1024)} %param.27) | copy-start | bytes 24580
  247.2 153.0 %all-gather.14.cloned.1.call-start = ((), (), s32[]{:S(2)}) async-start(), calls=%async_computation.4 | async-start | bytes 1114112 | tf_op jit(solution)/shard_map/all_gather | solution.py:117
  338.7 130.5 %all-gather.18.cloned.1.call-start = ((), (), s32[]{:S(2)}) async-start(), calls=%async_computation.6 | async-start | bytes 2228224 | tf_op jit(solution)/shard_map/all_gather | solution.py:95
  339.3 197.9 %all-gather.20.cloned.1.call-start = ((), (), s32[]{:S(2)}) async-start(), calls=%async_computation.7 | async-start | bytes 2162688 | tf_op jit(solution)/shard_map/all_gather | solution.py:128
  400.2 3.3 copy-start.3
  401.8 3.0 copy-start.10
  404.7 202.4 %all-gather.16.cloned.1.call-start = ((), (), s32[]{:S(2)}) async-start(), calls=%async_computation.5 | async-start | bytes 2162688 | tf_op jit(solution)/shard_map/all_gather | solution.py:127
  469.2 2.2 copy-start.2
  469.2 2.9 copy-start.11
  469.2 2.9 copy-start.13
Sparse Core Ops, SparseCore 0:
  11.0 65.5 all-gather.7
  81.4 64.8 all-gather.9
  149.0 66.9 all-gather.11
  247.3 89.7 reduce-scatter.3
  340.9 59.2 all-gather.13
  403.5 65.6 all-gather.17
  471.6 65.5 all-gather.19
  540.1 66.9 all-gather.15
where the time goes:
time: 652 us; the launch traced here: 650 us
  waiting for transfers between devices  550 us (84%)
  matrix products  52.6 us (8%)
  other arithmetic  28.4 us (4%)
  between operations  15.1 us (2%)
    unnamed x9, waiting for transfers between devices  91.1 us
    all_gather x1, waiting for transfers between devices, shards(): lax.all_gather(memory_keys, 'seq', axis=0, tiled=True)  70 us
    all_gather x1, waiting for transfers between devices, shards(): lax.all_gather(values_local, 'seq', axis=0, tiled=True)  69.8 us
    all_gather x1, waiting for transfers between devices, shards(): lax.all_gather(source_hidden, 'head', axis=1, tiled=True)  68.6 us
    all_gather x1, waiting for transfers between devices, shards(): lax.all_gather(memory_values, 'seq', axis=0, tiled=True)  64.2 us
    all_gather x1, waiting for transfers between devices, shards(): lax.all_gather(keys_local, 'seq', axis=0, tiled=True)  63.3 us
    all_gather x1, waiting for transfers between devices, shards(): lax.all_gather(target_hidden, 'head', axis=1, tiled=True)  62.5 us
    all_gather x1, waiting for transfers between devices, shards(): encoder_full = lax.all_gather(encoder_out, 'head', axis=1, tiled=True)  60.9 us
  transfers between devices with their start and end apart: 8, of which 8 were waited for; matrix products, arithmetic and copies ran while one was open for 2% of the time, Pallas kernels for 0%

commit v1 on v0

--- a/solution.py
+++ b/solution.py
@@ -103,7 +103,9 @@
     attended = folder(
         initial,
         (
-            lax.all_gather(keys_local, "seq", axis=0, tiled=True),
+            jnp.concatenate(
+                lax.all_to_all(jnp.stack([keys_local] * lax.axis_size("seq")), "seq", 0, 0), axis=0
+            ),
             lax.all_gather(values_local, "seq", axis=0, tiled=True),
         ),
         jnp.int32(0),

time: 652 us -> 603 us (0.925)
  waiting for transfers between devices: 550 us -> 492 us
  starting transfers between devices: 0.32 us -> 8.19 us
    all_gather x1 -> x0, waiting for transfers between devices: 63.3 us -> none  [shards(): lax.all_gather(keys_local, 'seq', axis=0, tiled=True)]
    all_to_all x0 -> x1, waiting for transfers between devices: none -> 53.1 us  [shards(): lax.all_to_all(jnp.stack([keys_local] * lax.axis_size('seq')), 'seq', 0, 0)]
    all_gather x1, waiting for transfers between devices: 69.8 us -> 22.4 us  [shards(): lax.all_gather(values_local, 'seq', axis=0, tiled=True)]
    all_to_all x0 -> x1, starting transfers between devices: none -> 7.91 us  [shards(): lax.all_to_all(jnp.stack([keys_local] * lax.axis_size('seq')), 'seq', 0, 0)]
    unnamed x9 -> x8, waiting for transfers between devices: 91.1 us -> 90.6 us
where the time goes in v1:
time: 603 us; the launch traced here: 601 us
  waiting for transfers between devices  492 us (82%)
  matrix products  52 us (9%)
  other arithmetic  28.4 us (5%)
  between operations  15.1 us (3%)
  starting transfers between devices  8.19 us (1%)
    unnamed x8, waiting for transfers between devices  90.6 us
    all_gather x1, waiting for transfers between devices, shards(): lax.all_gather(memory_keys, 'seq', axis=0, tiled=True)  70 us
    all_gather x1, waiting for transfers between devices, shards(): lax.all_gather(source_hidden, 'head', axis=1, tiled=True)  68.7 us
    all_gather x1, waiting for transfers between devices, shards(): lax.all_gather(memory_values, 'seq', axis=0, tiled=True)  64 us
    all_gather x1, waiting for transfers between devices, shards(): lax.all_gather(target_hidden, 'head', axis=1, tiled=True)  62.5 us
    all_gather x1, waiting for transfers between devices, shards(): encoder_full = lax.all_gather(encoder_out, 'head', axis=1, tiled=True)  60.9 us
    all_to_all x1, waiting for transfers between devices, shards(): lax.all_to_all(jnp.stack([keys_local] * lax.axis_size('seq')), 'seq', 0, 0)  53.1 us
    dot_general x16, matrix products, block_step(): jnp.einsum('hrk,khd->rhd', weights.astype(jnp.bfloat16), value_block, pre...  24.6 us
  transfers between devices with their start and end apart: 8, of which 8 were waited for; matrix products, arithmetic and copies ran while one was open for 2% of the time, Pallas kernels for 0%

profile of v1, /device:TPU:1, one launch (start us, length us, event | category | flops | bytes accessed | tf_op | source)
XLA Modules:
  0.0 601.2 jit_solution(15685094985052655761)
XLA Ops:
  7.9 68.7 %all-gather.7.cloned.1.call-done = bf16[256,2048]{1,0:T(8,128)(2,1)} async-done(((bf16[256,128]{1,0:T(8,128)(2,1)}), bf16[256,2048]{1,0:T(8,128)(2,1)}) %all-gather.7.cloned.1.call-update) | async-done | bytes 1048592 | tf_op jit(solution)/shard_map/all_gather | solution.py:94
  76.6 1.5 convert_reduce_fusion.2
  78.1 1.6 fusion.50
  80.6 1.8 stack.2
  82.5 7.9 %all-to-all-start = ((bf16[32,256,128]{2,1,0:T(8,128)(2,1)}), bf16[32,256,128]{2,1,0:T(8,128)(2,1)}, u32[]{:S(2)}, u32[]{:S(2)}) async-start(bf16[32,256,128]{2,1,0:T(8,128)(2,1)} %stack.2), calls=%async_computation | async-start | bytes 4194304 | tf_op jit(solution)/shard_map/all_to_all | solution.py:107
  92.0 53.1 %all-to-all-done = bf16[32,256,128]{2,1,0:T(8,128)(2,1)} async-done(((bf16[32,256,128]{2,1,0:T(8,128)(2,1)}), bf16[32,256,128]{2,1,0:T(8,128)(2,1)}, u32[]{:S(2)}, u32[]{:S(2)}) %all-to-all-start) | async-done | bytes 2097184 | tf_op jit(solution)/shard_map/all_to_all | solution.py:107
  145.2 22.4 %all-gather.9.cloned.1.call-done = bf16[8192,128]{1,0:T(8,128)(2,1)} async-done(((bf16[256,128]{1,0:T(8,128)(2,1)}), bf16[8192,128]{1,0:T(8,128)(2,1)}) %all-gather.9.cloned.1.call-update) | async-done | bytes 2097168 | tf_op jit(solution)/shard_map/all_gather | solution.py:109
  167.6 29.3 %while.36 = (s32[]{:T(128)}, f32[1,256]{1,0:T(1,128)S(1)}, f32[1,256]{1,0:T(1,128)S(1)}, f32[256,1,128]{0,2,1:T(8,128)S(1)}, s32[]{:T(128)}, /*index=5*/bf16[819...) while((s32[]{:T(128)}, f32[1,256]{1,0:T(1,128)S(1)}, ...), condition=%wide.region_5.6_spmd.clone, body=%wide.region_2.5_spmd.clone.sunk | while | flops 136678656 | bytes 4018367 | solution.py:61
  198.7 89.3 %reduce-scatter.4.cloned.1.call-done = bf16[128,256]{1,0:T(8,128)(2,1)} async-done(((bf16[2048,256]{1,0:T(8,128)(2,1)}), bf16[128,256]{1,0:T(8,128)(2,1)}) %reduce-scatter.4.cloned.1.call-update) | async-done | bytes 65552
  290.3 60.9 %all-gather.11.cloned.1.call-done = bf16[256,2048]{1,0:T(8,128)(2,1)} async-done(((bf16[256,128]{1,0:T(8,128)(2,1)}), bf16[256,2048]{1,0:T(8,128)(2,1)}) %all-gather.11.cloned.1.call-update) | async-done | bytes 1048592 | tf_op jit(solution)/shard_map/all_gather | solution.py:119
  352.7 1.7 fusion.47
  357.6 62.5 %all-gather.15.cloned.1.call-done = bf16[512,2048]{1,0:T(8,128)(2,1)} async-done(((bf16[512,128]{1,0:T(8,128)(2,1)}), bf16[512,2048]{1,0:T(8,128)(2,1)}) %all-gather.15.cloned.1.call-update) | async-done | bytes 2097168 | tf_op jit(solution)/shard_map/all_gather | solution.py:95
  420.1 2.1 convert_reduce_fusion
  423.9 64.0 %all-gather.17.cloned.1.call-done = bf16[8192,128]{1,0:T(8,128)(2,1)} async-done(((bf16[256,128]{1,0:T(8,128)(2,1)}), bf16[8192,128]{1,0:T(8,128)(2,1)}) %all-gather.17.cloned.1.call-update) | async-done | bytes 2097168 | tf_op jit(solution)/shard_map/all_gather | solution.py:130
  487.9 70.0 %all-gather.13.cloned.1.call-done = bf16[8192,128]{1,0:T(8,128)(2,1)} async-done(((bf16[256,128]{1,0:T(8,128)(2,1)}), bf16[8192,128]{1,0:T(8,128)(2,1)}) %all-gather.13.cloned.1.call-update) | async-done | bytes 2097168 | tf_op jit(solution)/shard_map/all_gather | solution.py:129
  557.9 35.4 %while.37 = (s32[]{:T(128)}, f32[1,512]{1,0:T(1,128)S(1)}, f32[1,512]{1,0:T(1,128)S(1)}, f32[512,1,128]{0,2,1:T(8,128)S(1)}, s32[]{:T(128)}, /*index=5*/bf16[819...) while((s32[]{:T(128)}, f32[1,512]{1,0:T(1,128)S(1)}, ...), condition=%wide.region_14.15_spmd.clone, body=%wide.region_11.14_spmd.clone.sunk | while | flops 275452416 | bytes 7508159 | solution.py:61
  560.6 1.7 fusion.107
  565.0 1.7 fusion.107
  569.5 1.7 fusion.107
  573.9 1.7 fusion.107
  578.3 1.7 fusion.107
  582.8 1.7 fusion.107
  587.2 1.7 fusion.107
  591.6 1.7 fusion.107
  (174 shorter events, 64.0 us)
Async XLA Ops:
  7.2 189.7 %copy-start = (bf16[128,2048]{1,0:T(8,128)(2,1)S(1)}, bf16[128,2048]{1,0:T(8,128)(2,1)}, u32[]{:S(2)}) copy-start(bf16[128,2048]{1,0:T(8,128)(2,1)} %param.26) | copy-start | bytes 1572868
  7.2 72.6 %copy-start.8 = (f32[2048]{0:T(1024)S(1)}, f32[2048]{0:T(1024)}, u32[]{:S(2)}) copy-start(f32[2048]{0:T(1024)} %param.22) | copy-start | bytes 24580
  7.2 69.4 %all-gather.7.cloned.1.call-start = ((), (), s32[]{:S(2)}) async-start(), calls=%async_computation.2 | async-start | bytes 1114112 | tf_op jit(solution)/shard_map/all_gather | solution.py:94
  7.9 72.3 %copy-start.4 = (bf16[2048,128]{1,0:T(8,128)(2,1)S(1)}, bf16[2048,128]{1,0:T(8,128)(2,1)}, u32[]{:S(2)}) copy-start(bf16[2048,128]{1,0:T(8,128)(2,1)} %param.24) | copy-start | bytes 1572868
  76.6 3.2 copy-start.1
  82.5 8.0 %copy-start.5 = (bf16[2048,128]{1,0:T(8,128)(2,1)S(1)}, bf16[2048,128]{1,0:T(8,128)(2,1)}, u32[]{:S(2)}) copy-start(bf16[2048,128]{1,0:T(8,128)(2,1)} %param.25) | copy-start | bytes 1572868
  82.5 9.1 %copy-start.6 = (bf16[2048,128]{1,0:T(8,128)(2,1)S(1)}, bf16[2048,128]{1,0:T(8,128)(2,1)}, u32[]{:S(2)}) copy-start(bf16[2048,128]{1,0:T(8,128)(2,1)} %param.23) | copy-start | bytes 1572868
  82.5 62.7 %all-to-all-start = ((bf16[32,256,128]{2,1,0:T(8,128)(2,1)}), bf16[32,256,128]{2,1,0:T(8,128)(2,1)}, u32[]{:S(2)}, u32[]{:S(2)}) async-start(bf16[32,256,128]{2,1,0:T(8,128)(2,1)} %stack.2), calls=%async_computation | async-start | bytes 4194304 | tf_op jit(solution)/shard_map/all_to_all | solution.py:107
  90.4 77.2 %all-gather.9.cloned.1.call-start = ((), (), s32[]{:S(2)}) async-start(), calls=%async_computation.3 | async-start | bytes 2162688 | tf_op jit(solution)/shard_map/all_gather | solution.py:109
  91.5 196.5 %reduce-scatter.4.cloned.1.call-start = ((), (), s32[]{:S(2)}) async-start(), calls=%async_computation.8 | async-start | bytes 1114112
  196.9 92.1 %copy-start.7 = (bf16[256,128]{1,0:T(8,128)(2,1)S(1)}, bf16[256,128]{1,0:T(8,128)(2,1)}, u32[]{:S(2)}) copy-start(bf16[256,128]{1,0:T(8,128)(2,1)} %param.18) | copy-start | bytes 196612
  198.6 155.8 %copy-start.9 = (bf16[2048,128]{1,0:T(8,128)(2,1)S(1)}, bf16[2048,128]{1,0:T(8,128)(2,1)}, u32[]{:S(2)}) copy-start(bf16[2048,128]{1,0:T(8,128)(2,1)} %param.30) | copy-start | bytes 1572868
  198.6 155.8 %copy-start.12 = (f32[2048]{0:T(1024)S(1)}, f32[2048]{0:T(1024)}, u32[]{:S(2)}) copy-start(f32[2048]{0:T(1024)} %param.27) | copy-start | bytes 24580
  198.7 152.5 %all-gather.11.cloned.1.call-start = ((), (), s32[]{:S(2)}) async-start(), calls=%async_computation.4 | async-start | bytes 1114112 | tf_op jit(solution)/shard_map/all_gather | solution.py:119
  289.6 130.5 %all-gather.15.cloned.1.call-start = ((), (), s32[]{:S(2)}) async-start(), calls=%async_computation.6 | async-start | bytes 2228224 | tf_op jit(solution)/shard_map/all_gather | solution.py:95
  290.2 197.7 %all-gather.17.cloned.1.call-start = ((), (), s32[]{:S(2)}) async-start(), calls=%async_computation.7 | async-start | bytes 2162688 | tf_op jit(solution)/shard_map/all_gather | solution.py:130
  351.1 3.3 copy-start.3
  352.7 3.0 copy-start.10
  355.6 202.2 %all-gather.13.cloned.1.call-start = ((), (), s32[]{:S(2)}) async-start(), calls=%async_computation.5 | async-start | bytes 2162688 | tf_op jit(solution)/shard_map/all_gather | solution.py:129
  420.1 2.2 copy-start.2
  420.1 2.9 copy-start.11
  420.1 2.9 copy-start.13
Sparse Core Ops, SparseCore 0:
  11.0 65.5 all-gather.6
  93.9 73.5 all-gather.8
  198.8 89.1 reduce-scatter.3
  291.8 59.2 all-gather.10
  354.4 65.6 all-gather.14
  422.3 65.5 all-gather.16
  490.8 66.9 all-gather.12
